TPU v7x, 32 devices: a whole 2x2x4 slice. The times are simulated.
32 devices in a mesh: seq: 16 (over z, x, core), ch: 2 (over y).
Axes of the slice: x: 2, y: 2, z: 4, core: 2. Of those that a mesh axis runs over, the one named last changes fastest.
Arguments:
- q_proj: bfloat16 [4096, 8192], P('seq', 'ch'), may hold values from -60 to 60
- k_proj: bfloat16 [4096, 8192], P('seq', 'ch'), may hold values from -6 to 6
- v_proj: bfloat16 [4096, 8192], P('seq', 'ch'), may hold values from -6 to 6
- short_filter: float32 [9, 8192], P(None, 'ch'), may hold values from -3 to 3
- log_decay: float32 [512, 16], P('ch'), may hold values from -0.1 to -0.00012207031
- residue: float32 [512, 16], P('ch'), may hold values from -15 to 15
- skip_bias: float32 [8192], P('ch'), may hold values from -4 to 4
- norm_gain: float32 [8192], P('ch'), may hold values from 0.25 to 1.75
Outputs:
- mixed_out: bfloat16 [4096, 8192], P('seq', 'ch')
All inputs are finite; a program needn't handle non-finite values.
Results may differ from a plain program's by a relative error of at most 0.0058.
Values may be sent and summed in bfloat16 or wider, within the bound.
A program may use at most 128 MiB of HBM per device.

v0:
```python
import functools
import jax
import jax.numpy as jnp
from jax import lax
from jax.experimental import pallas as pl
from jax.experimental.pallas import tpu as pltpu
from jax.sharding import PartitionSpec as P

LANES = 128
MESH = pl.DeviceIdType.MESH
f32 = jnp.float32
bf16 = jnp.bfloat16


def tile_at(i):
    return pl.ds(pl.multiple_of(i * LANES, LANES), LANES)


def kernel(n, nch, rounds, modes, q_hbm, k_hbm, v_hbm, taps_hbm, decay_hbm, residue_hbm, skip_hbm, gain_hbm,
           out_ref, q_ref, k_ref, v_ref, taps_ref, decay_flat, residue_flat, skip_ref, gain_ref,
           tails, decay_ref, residue_ref, halo_out, halo_in, pad, leaving, hrev, entering, mixed, conv, rate, wide_weight,
           total, carry, carry_in, first_out, first_in, state_out, state_in, square, square_out, square_in,
           halo_send, halo_recv, state_send, state_recv, square_send, square_recv, load_sem, tail_sem, carry_send, carry_recv):
    tok, channels = q_ref.shape
    half = tok // 2
    tiles = channels // LANES
    per = LANES // modes
    me = lax.axis_index("seq")
    mych = lax.axis_index("ch")
    right, left = lax.rem(me + 1, n), lax.rem(me + n - 1, n)

    def partner(bit):
        return me + bit * (1 - 2 * lax.rem(lax.div(me, bit), 2))

    def scan_copy(r):
        return pltpu.make_async_remote_copy(
            state_out.at[r] if r else first_out, state_in.at[r] if r else first_in, state_send.at[r], state_recv.at[r],
            device_id={"seq": partner(1 << r)}, device_id_type=MESH)

    order = ((decay_hbm, decay_flat), (residue_hbm, residue_flat), (k_hbm, k_ref), (v_hbm, v_ref), (taps_hbm, taps_ref),
             (skip_hbm, skip_ref), (q_hbm, q_ref), (gain_hbm, gain_ref))
    tail_loads = [pltpu.make_async_copy(ref.at[tok - 16:tok, :], tails.at[j], tail_sem.at[j])
                  for j, ref in enumerate((q_hbm, k_hbm, v_hbm))]
    loads = [pltpu.make_async_copy(src, dst, load_sem.at[j]) for j, (src, dst) in enumerate(order)]
    for load in tail_loads + loads:
        load.start()
    barrier = pltpu.get_barrier_semaphore()
    for other in [right, left] + [partner(1 << r) for r in range(rounds)]:
        pl.semaphore_signal(barrier, inc=1, device_id={"seq": other}, device_id_type=MESH)
    for d in range(1, nch):
        pl.semaphore_signal(barrier, inc=1, device_id={"ch": lax.rem(mych + d, nch)}, device_id_type=MESH)

    halo_out[...] = jnp.zeros_like(halo_out)
    for j in range(3):
        tail_loads[j].wait()
        halo_out[2 * j:2 * j + 2, :] = tails[j].astype(f32)[14:16]
    pl.semaphore_wait(barrier, 2 + rounds + nch - 1)

    halo = pltpu.make_async_remote_copy(halo_out, halo_in, halo_send, halo_recv,
                                        device_id={"seq": right}, device_id_type=MESH)

    @pl.when(me < n - 1)
    def _():
        halo.start()

    lane = lax.broadcasted_iota(jnp.int32, (1, LANES), 1)
    lane_group = lane // modes
    lags_rev = (tok - 1 - lax.broadcasted_iota(jnp.int32, (1, tok), 1)).astype(f32)

    spread = (lax.broadcasted_iota(jnp.int32, (modes, LANES), 1) % modes
              == lax.broadcasted_iota(jnp.int32, (modes, LANES), 0)).astype(f32)
    after = (lax.broadcasted_iota(jnp.int32, (tok, 1), 0) + 1).astype(f32)
    sub = lax.broadcasted_iota(jnp.int32, (per, LANES), 0)
    sub_lane = lax.broadcasted_iota(jnp.int32, (per, LANES), 1) // modes

    def prepare(i, _):
        logs = decay_ref[pl.ds(pl.multiple_of(i * per, per), per), :]
        res = residue_ref[pl.ds(pl.multiple_of(i * per, per), per), :]
        pole = jnp.exp(logs)
        weight = res * jnp.sqrt(1.0 - pole * pole)
        cols, wcols = logs.T, weight.T
        rows = []
        wide_rate = jnp.zeros((modes, LANES), f32)
        wide_w = jnp.zeros((modes, LANES), f32)
        for j in range(per):
            col, wcol = cols[:, j:j + 1], wcols[:, j:j + 1]
            power = jnp.exp(col * lags_rev)
            leaving[pl.ds(pl.multiple_of(i * LANES, LANES) + j * modes, modes), :] = power.astype(bf16)
            rows.append(jnp.sum(power * wcol, axis=0, keepdims=True))
            wide_rate = jnp.where(lane_group == j, col, wide_rate)
            wide_w = jnp.where(lane_group == j, wcol, wide_w)
        hrev[pl.ds(pl.multiple_of(i * per, per), per), :] = jnp.concatenate(rows, axis=0)
        rate[:, tile_at(i)] = wide_rate
        wide_weight[:, tile_at(i)] = wide_w
        return 0

    loads[0].wait()
    loads[1].wait()
    decay_ref[...] = decay_flat[...].T
    residue_ref[...] = residue_flat[...].T
    lax.fori_loop(0, tiles, prepare, 0)
    for load in loads[2:6]:
        load.wait()

    @pl.when(me > 0)
    def _():
        halo.wait_recv()

    @pl.when(me == 0)
    def _():
        halo_in[...] = jnp.zeros_like(halo_in)

    def short(ref, which, i, slot=0):
        place = 3 * slot + which
        pad[place, 8:8 + tok, :] = ref[:, tile_at(i)].astype(f32)
        pad[place, 0:8, :] = jnp.concatenate(
            [jnp.zeros((6, LANES), f32), halo_in[2 * which:2 * which + 2, tile_at(i)]], axis=0)
        a = [taps_ref[3 * which + t:3 * which + t + 1, tile_at(i)] for t in range(3)]
        return a[0] * pad[place, 8:8 + tok, :] + a[1] * pad[place, 7:7 + tok, :] + a[2] * pad[place, 6:6 + tok, :]

    def summarize(i, _):
        pair = [2 * i, 2 * i + 1]
        values = [(short(k_ref, 1, t, u) * short(v_ref, 2, t, u)).astype(bf16) for u, t in enumerate(pair)]
        spreadout = [jnp.dot(leaving[tile_at(t), :], values[u], preferred_element_type=f32) for u, t in enumerate(pair)]
        for u, t in enumerate(pair):
            state = jnp.zeros((modes, LANES), f32)
            for j in range(per):
                state = jnp.where(lane_group == j, spreadout[u][j * modes:(j + 1) * modes], state)
            mixed[:, tile_at(t)] = values[u]
            total[:, tile_at(t)] = state
            first_out[:, tile_at(t)] = state.astype(bf16)
        return 0

    lax.fori_loop(0, tiles // 2, summarize, 0)

    causal = (lax.broadcasted_iota(jnp.int32, (half, tok), 1)
              <= lax.broadcasted_iota(jnp.int32, (half, tok), 0) + half)

    def convolve(i, _):
        values = mixed[:, tile_at(i)]
        first, second = values[:half], values[half:]
        right_side = jnp.concatenate(
            [jnp.concatenate([jnp.zeros_like(first), first], axis=1),
             jnp.concatenate([first, second], axis=1)], axis=0)
        lines = hrev[pl.ds(pl.multiple_of(i * per, per), per), :]
        blocks = []
        for j in range(per):
            line = jnp.broadcast_to(lines[j:j + 1], (half, tok))
            block = pltpu.roll(line, half + 1, 1, stride=1, stride_axis=0)
            blocks.append(jnp.where(causal, block, 0.0).astype(bf16))
        product = jnp.dot(jnp.concatenate(blocks, axis=0), right_side, preferred_element_type=f32)
        low = jnp.zeros((half, LANES), f32)
        high = jnp.zeros((half, LANES), f32)
        for j in range(per):
            part = product[j * half:(j + 1) * half]
            low = jnp.where(lane_group == j, part[:, :LANES], low)
            high = jnp.where(lane_group == j, part[:, LANES:], high)
        skip = skip_ref[:, tile_at(i)]
        conv[:half, tile_at(i)] = low + skip * first.astype(f32)
        conv[half:, tile_at(i)] = high + skip * second.astype(f32)
        logs = decay_ref[pl.ds(pl.multiple_of(i * per, per), per), :]
        row = jnp.dot(logs, spread, preferred_element_type=f32, precision=lax.Precision.HIGHEST)
        row = jnp.sum(jnp.where(sub == sub_lane, row, 0.0), axis=0, keepdims=True)
        entering[:, tile_at(i)] = jnp.exp(after * row).astype(bf16)
        q_ref[:, tile_at(i)] = short(q_ref, 0, i).astype(bf16)
        return 0

    loads[6].wait()

    carry[...] = jnp.zeros_like(carry)
    half_tiles = tiles // 2
    core = lax.rem(me, 2)
    lead = max(tiles // 8, 1)
    tail = max(tiles // 16, 1)
    bounds = [0] + [lead + (tiles - lead - tail) * r // (rounds - 1) for r in range(rounds)]
    for r in range(rounds):
        bit = 1 << r
        last = r == rounds - 1
        upper = lax.rem(lax.div(me, bit), 2) == 1
        copy = scan_copy(r)
        if last:
            @pl.when(jnp.logical_not(upper))
            def _():
                copy.start()
        else:
            copy.start()
        lax.fori_loop(bounds[r], bounds[r + 1], convolve, 0)
        block_rate = float(tok * bit)
        offset = ((lax.rem(me, bit) - core) * tok).astype(f32) if r else None

        def merge(i, _):
            place = tile_at(core * half_tiles + i)
            theirs = (state_in[r, :, tile_at(i)] if r else first_in[:, place]).astype(f32)
            logs = rate[:, place]
            if r:
                inward = jnp.exp(logs * offset) * theirs
                carry[:, tile_at(i)] += jnp.where(upper, inward, 0.0)
            if not last:
                mine = total[:, place]
                later = jnp.where(upper, mine, theirs)
                before = jnp.where(upper, theirs, mine)
                both = jnp.exp(logs * block_rate) * before + later
                total[:, place] = both
                state_out[r + 1, :, tile_at(i)] = both.astype(bf16)
            return 0

        if last:
            @pl.when(upper)
            def _():
                copy.wait_recv()
                lax.fori_loop(0, half_tiles, merge, 0)
        else:
            copy.wait_recv()
            lax.fori_loop(0, half_tiles, merge, 0)

    share = pltpu.make_async_remote_copy(carry, carry_in, carry_send, carry_recv,
                                         device_id={"seq": partner(1)}, device_id_type=MESH)
    share.start()
    lax.fori_loop(bounds[rounds], tiles, convolve, 0)
    share.wait()

    def assemble(i, _):
        for part, side in ((carry, core), (carry_in, 1 - core)):
            place = tile_at(side * half_tiles + i)
            entry = part[:, tile_at(i)]
            moved = jnp.exp(rate[:, place] * float(tok)) * entry + first_in[:, place].astype(f32)
            total[:, place] = jnp.where(core == 1, moved, entry)
        return 0

    lax.fori_loop(0, half_tiles, assemble, 0)

    square[...] = jnp.zeros_like(square)
    loads[7].wait()

    def gated_tile(i):
        state = total[:, tile_at(i)] * wide_weight[:, tile_at(i)]
        diagonal = jnp.concatenate([jnp.where(lane_group == j, state, 0.0) for j in range(per)], axis=0)
        fine = diagonal.astype(bf16)
        rest = (diagonal - fine.astype(f32)).astype(bf16)
        ent = entering[:, tile_at(i)]
        carried = jnp.dot(jnp.concatenate([ent, ent], axis=1), jnp.concatenate([fine, rest], axis=0),
                          preferred_element_type=f32)
        return q_ref[:, tile_at(i)].astype(f32) * (conv[:, tile_at(i)] + carried)

    def gate(i, _):
        one, two = gated_tile(2 * i), gated_tile(2 * i + 1)
        conv[:, tile_at(2 * i)] = one
        conv[:, tile_at(2 * i + 1)] = two
        square[...] += one * one + two * two
        return 0

    lax.fori_loop(0, tiles // 2, gate, 0)

    sums = jnp.sum(square[...].T, axis=0, keepdims=True)
    square_out[...] = jnp.broadcast_to(sums, square_out.shape)
    copies = []
    for d in range(1, nch):
        c = pltpu.make_async_remote_copy(square_out, square_in.at[d - 1], square_send.at[d - 1], square_recv.at[d - 1],
                                         device_id={"ch": lax.rem(mych + d, nch)}, device_id_type=MESH)
        c.start()
        copies.append(c)
    for d, c in enumerate(copies):
        c.wait()
        sums = sums + square_in[d, 0:1, :]
    scale = lax.rsqrt(sums / (channels * nch) + 1e-5)
    square[...] = jnp.broadcast_to(scale, (LANES, tok)).T

    def finish(i, _):
        out_ref[:, tile_at(i)] = (conv[:, tile_at(i)] * square[...] * gain_ref[:, tile_at(i)]).astype(bf16)
        return 0

    lax.fori_loop(0, tiles, finish, 0)

    @pl.when(me < n - 1)
    def _():
        halo.wait_send()

    for r in range(rounds):
        bit = 1 << r
        copy = scan_copy(r)
        if r == rounds - 1:
            @pl.when(lax.rem(lax.div(me, bit), 2) == 0)
            def _():
                copy.wait_send()
        else:
            copy.wait_send()


def on_device(n, nch, q_proj, k_proj, v_proj, short_filter, log_decay, residue, skip_bias, norm_gain):
    tok, channels = q_proj.shape
    groups, modes = log_decay.shape
    rounds = n.bit_length() - 1
    assert channels % (2 * LANES) == 0 and n == 1 << rounds and rounds > 1 and channels == groups * modes
    vmem = pl.BlockSpec(memory_space=pltpu.VMEM)
    dma = pltpu.SemaphoreType.DMA
    return pl.pallas_call(
        functools.partial(kernel, n, nch, rounds, modes),
        out_shape=jax.ShapeDtypeStruct((tok, channels), bf16),
        in_specs=[pl.BlockSpec(memory_space=pltpu.HBM)] * 8,
        out_specs=vmem,
        scratch_shapes=[
            pltpu.VMEM((tok, channels), bf16),
            pltpu.VMEM((tok, channels), bf16),
            pltpu.VMEM((tok, channels), bf16),
            pltpu.VMEM((9, channels), f32),
            pltpu.VMEM((modes, groups), f32),
            pltpu.VMEM((modes, groups), f32),
            pltpu.VMEM((1, channels), f32),
            pltpu.VMEM((1, channels), f32),
            pltpu.VMEM((3, 16, channels), bf16),
            pltpu.VMEM((groups, modes), f32),
            pltpu.VMEM((groups, modes), f32),
            pltpu.VMEM((8, channels), f32),
            pltpu.VMEM((8, channels), f32),
            pltpu.VMEM((6, tok + 8, LANES), f32),
            pltpu.VMEM((channels, tok), bf16),
            pltpu.VMEM((groups, tok), f32),
            pltpu.VMEM((tok, channels), bf16),
            pltpu.VMEM((tok, channels), bf16),
            pltpu.VMEM((tok, channels), f32),
            pltpu.VMEM((modes, channels), f32),
            pltpu.VMEM((modes, channels), f32),
            pltpu.VMEM((modes, channels), f32),
            pltpu.VMEM((modes, channels // 2), f32),
            pltpu.VMEM((modes, channels // 2), f32),
            pltpu.VMEM((modes, channels), bf16),
            pltpu.VMEM((modes, channels), bf16),
            pltpu.VMEM((rounds, modes, channels // 2), bf16),
            pltpu.VMEM((rounds, modes, channels // 2), bf16),
            pltpu.VMEM((tok, LANES), f32),
            pltpu.VMEM((8, tok), f32),
            pltpu.VMEM((max(nch - 1, 1), 8, tok), f32),
            dma, dma, dma((rounds,)), dma((rounds,)), dma((max(nch - 1, 1),)), dma((max(nch - 1, 1),)),
            dma((8,)), dma((3,)), dma, dma,
        ],
        compiler_params=pltpu.CompilerParams(collective_id=0, has_side_effects=True,
                                             vmem_limit_bytes=50 * 1024 * 1024),
    )(q_proj, k_proj, v_proj, short_filter, log_decay.T, residue.T,
      skip_bias.reshape(1, channels), norm_gain.reshape(1, channels))


def solution(mesh):
    return jax.shard_map(
        functools.partial(on_device, mesh.shape["seq"], mesh.shape["ch"]),
        mesh=mesh,
        in_specs=(P("seq", "ch"), P("seq", "ch"), P("seq", "ch"), P(None, "ch"),
                  P("ch", None), P("ch", None), P("ch"), P("ch")),
        out_specs=P("seq", "ch"),
        check_vma=False,
    )
```

profile of v0, /device:TPU:0, one launch (start us, length us, event | category | flops | bytes accessed | tf_op | source)
XLA Modules:
  0.0 47.4 jit_solution(7223506549766850407)
XLA Ops:
  0.0 0.0 copy-start
  0.0 0.9 %copy-done = f32[9,4096]{1,0:T(8,128)S(1)} copy-done((f32[9,4096]{1,0:T(8,128)S(1)}, f32[9,4096]{1,0:T(8,128)}, u32[]{:S(2)}) %copy-start) | copy-done | bytes 147480
  1.0 0.0 copy-start.1
  1.0 0.7 %copy-done.1 = f32[256,16]{0,1:T(8,128)S(1)} copy-done((f32[256,16]{0,1:T(8,128)S(1)}, f32[256,16]{0,1:T(8,128)}, u32[]{:S(2)}) %copy-start.1) | copy-done | bytes 16408
  1.7 0.0 copy-start.2
  1.7 0.7 %copy-done.2 = f32[256,16]{0,1:T(8,128)S(1)} copy-done((f32[256,16]{0,1:T(8,128)S(1)}, f32[256,16]{0,1:T(8,128)}, u32[]{:S(2)}) %copy-start.2) | copy-done | bytes 16408
  2.4 0.0 copy-start.3
  2.4 0.7 %copy-done.3 = f32[4096]{0:T(1024)S(1)} copy-done((f32[4096]{0:T(1024)S(1)}, f32[4096]{0:T(1024)}, u32[]{:S(2)}) %copy-start.3) | copy-done | bytes 16408
  3.1 0.0 copy-start.4
  3.1 0.7 %copy-done.4 = f32[4096]{0:T(1024)S(1)} copy-done((f32[4096]{0:T(1024)S(1)}, f32[4096]{0:T(1024)}, u32[]{:S(2)}) %copy-start.4) | copy-done | bytes 16408
  3.8 42.3 %shard_map.82 = bf16[256,4096]{1,0:T(8,128)(2,1)S(1)} custom-call(bf16[256,4096]{1,0:T(8,128)(2,1)} %q_hbm.1, bf16[256,4096]{1,0:T(8,128)(2,1)} %k_hbm.1, bf16[256,4096]{1,0:T(8,128)(2,1)} %v_hbm.1, f32[9,4096]{1,0:T(8,128)S(1)} %copy-done, f32[16,256]{1,0:T(8,128)S(1)} %bitcast.4, f32[16,256]{1,0:T(8,128)S(1)} %bitcast.5, f32[1,4096]{1,0:T(1,128)S(1)} %bitcast.6, ...), custom_call_target="tpu_custom_call" | custom-call | tf_op jit(solution)/shard_map/pallas_call | solution.py:296
  46.1 1.3 %copy.10 = bf16[256,4096]{1,0:T(8,128)(2,1)} copy(bf16[256,4096]{1,0:T(8,128)(2,1)S(1)} %shard_map.82) | data formatting | bytes 4194304
Async XLA Ops:
  0.0 0.9 %copy-start = (f32[9,4096]{1,0:T(8,128)S(1)}, f32[9,4096]{1,0:T(8,128)}, u32[]{:S(2)}) copy-start(f32[9,4096]{1,0:T(8,128)} %taps_hbm.1) | copy-start | bytes 442372
  1.0 0.7 %copy-start.1 = (f32[256,16]{0,1:T(8,128)S(1)}, f32[256,16]{0,1:T(8,128)}, u32[]{:S(2)}) copy-start(f32[256,16]{0,1:T(8,128)} %param.12) | copy-start | bytes 49156
  1.7 0.7 %copy-start.2 = (f32[256,16]{0,1:T(8,128)S(1)}, f32[256,16]{0,1:T(8,128)}, u32[]{:S(2)}) copy-start(f32[256,16]{0,1:T(8,128)} %param.13) | copy-start | bytes 49156
  2.4 0.7 %copy-start.3 = (f32[4096]{0:T(1024)S(1)}, f32[4096]{0:T(1024)}, u32[]{:S(2)}) copy-start(f32[4096]{0:T(1024)} %param.14) | copy-start | bytes 49156
  3.1 0.7 %copy-start.4 = (f32[4096]{0:T(1024)S(1)}, f32[4096]{0:T(1024)}, u32[]{:S(2)}) copy-start(f32[4096]{0:T(1024)} %param.15) | copy-start | bytes 49156
where the time goes:
time: 47.9 us; the launch traced here: 47.4 us
  Pallas kernels  42.3 us (88%)
  local copies, waits for them, and re-layouts  5.14 us (11%)
    pallas_call x1, Pallas kernels, on_device(): pl.pallas_call(functools.partial(kernel, n, nch, rounds, modes), out_shap...  42.3 us
    unnamed x11, local copies, waits for them, and re-layouts  5.14 us

commit v1 on v0

--- a/solution.py
+++ b/solution.py
@@ -334,7 +334,7 @@
             dma((8,)), dma((3,)), dma, dma,
         ],
         compiler_params=pltpu.CompilerParams(collective_id=0, has_side_effects=True,
-                                             vmem_limit_bytes=50 * 1024 * 1024),
+                                             vmem_limit_bytes=56 * 1024 * 1024),
     )(q_proj, k_proj, v_proj, short_filter, log_decay.T, residue.T,
       skip_bias.reshape(1, channels), norm_gain.reshape(1, channels))
 

time: 47.9 us -> 46.8 us (0.977)
  local copies, waits for them, and re-layouts: 5.14 us -> 3.13 us
  Pallas kernels: 42.3 us -> 43.5 us
    unnamed x11 -> x1, local copies, waits for them, and re-layouts: 5.14 us -> 3.13 us
    pallas_call x1, Pallas kernels: 42.3 us -> 43.5 us  [on_device(): pl.pallas_call(functools.partial(kernel, n, nch, rounds, modes), out_shap...]
where the time goes in v1:
time: 46.8 us; the launch traced here: 46.7 us
  Pallas kernels  43.5 us (93%)
  local copies, waits for them, and re-layouts  3.13 us (7%)
    pallas_call x1, Pallas kernels, on_device(): pl.pallas_call(functools.partial(kernel, n, nch, rounds, modes), out_shap...  43.5 us
    unnamed x1, local copies, waits for them, and re-layouts  3.13 us

profile of v1, /device:TPU:0, one launch (start us, length us, event | category | flops | bytes accessed | tf_op | source)
XLA Modules:
  0.0 46.7 jit_solution(1004971187515609303)
XLA Ops:
  0.0 43.5 %shard_map.82 = bf16[256,4096]{1,0:T(8,128)(2,1)} custom-call(bf16[256,4096]{1,0:T(8,128)(2,1)} %q_hbm.1, bf16[256,4096]{1,0:T(8,128)(2,1)} %k_hbm.1, bf16[256,4096]{1,0:T(8,128)(2,1)} %v_hbm.1, f32[9,4096]{1,0:T(8,128)} %taps_hbm.1, f32[16,256]{1,0:T(8,128)} %bitcast.4, f32[16,256]{1,0:T(8,128)} %bitcast.5, f32[1,4096]{1,0:T(1,128)} %bitcast.6, ...), custom_call_target="tpu_custom_call" | custom-call | tf_op jit(solution)/shard_map/pallas_call | solution.py:296
  43.5 3.1 %copy.10 = bf16[256,4096]{1,0:T(8,128)(2,1)} copy(bf16[256,4096]{1,0:T(8,128)(2,1)} %shard_map.82) | data formatting | bytes 4194304

commit v2 on v1

v2 whole, which is shorter than its diff:
```python
import functools
import jax
import jax.numpy as jnp
from jax import lax
from jax.experimental import pallas as pl
from jax.experimental.pallas import tpu as pltpu
from jax.sharding import PartitionSpec as P

LANES = 128
PARTS = 2
MESH = pl.DeviceIdType.MESH
f32 = jnp.float32
bf16 = jnp.bfloat16


def tile_at(i):
    return pl.ds(pl.multiple_of(i * LANES, LANES), LANES)


def kernel(n, nch, rounds, modes, q_hbm, k_hbm, v_hbm, taps_hbm, decay_hbm, residue_hbm, skip_hbm,
           conv, square, q_ref, k_ref, v_ref, taps_ref, decay_flat, residue_flat, skip_ref,
           tails, decay_ref, residue_ref, halo_out, halo_in, pad, leaving, hrev, entering, mixed, rate, wide_weight,
           total, first_half, carry, carry_in, first_out, first_in, state_out, state_in, square_out, square_in,
           halo_send, halo_recv, state_send, state_recv, square_send, square_recv, load_sem, tail_sem, carry_send, carry_recv):
    tok, channels = q_ref.shape
    half = tok // 2
    tiles = channels // LANES
    part_tiles = tiles // PARTS
    half_tiles = part_tiles // 2
    per = LANES // modes
    me = lax.axis_index("seq")
    mych = lax.axis_index("ch")
    right, left = lax.rem(me + 1, n), lax.rem(me + n - 1, n)

    def partner(bit):
        return me + bit * (1 - 2 * lax.rem(lax.div(me, bit), 2))

    def scan_copy(p, r):
        return pltpu.make_async_remote_copy(
            state_out.at[p, r] if r else first_out.at[p], state_in.at[p, r] if r else first_in.at[p],
            state_send.at[p, r], state_recv.at[p, r], device_id={"seq": partner(1 << r)}, device_id_type=MESH)

    def share_copy(p):
        return pltpu.make_async_remote_copy(carry.at[p], carry_in.at[p], carry_send.at[p], carry_recv.at[p],
                                            device_id={"seq": partner(1)}, device_id_type=MESH)

    order = ((decay_hbm, decay_flat), (residue_hbm, residue_flat), (k_hbm, k_ref), (v_hbm, v_ref), (taps_hbm, taps_ref),
             (skip_hbm, skip_ref), (q_hbm, q_ref))
    tail_loads = [pltpu.make_async_copy(ref.at[tok - 16:tok, :], tails.at[j], tail_sem.at[j])
                  for j, ref in enumerate((q_hbm, k_hbm, v_hbm))]
    loads = [pltpu.make_async_copy(src, dst, load_sem.at[j]) for j, (src, dst) in enumerate(order)]
    for load in tail_loads + loads:
        load.start()
    barrier = pltpu.get_barrier_semaphore()
    for other in [right, left] + [partner(1 << r) for r in range(rounds)]:
        pl.semaphore_signal(barrier, inc=1, device_id={"seq": other}, device_id_type=MESH)
    for d in range(1, nch):
        pl.semaphore_signal(barrier, inc=1, device_id={"ch": lax.rem(mych + d, nch)}, device_id_type=MESH)

    for load in tail_loads:
        load.wait()

    def make_halo(i, _):
        last = [tails[j, :, tile_at(i)].astype(f32)[14:16] for j in range(3)]
        halo_out[:, tile_at(i)] = jnp.concatenate(last + [jnp.zeros((2, LANES), f32)], axis=0).astype(bf16)
        return 0

    lax.fori_loop(0, tiles, make_halo, 0, unroll=4)
    pl.semaphore_wait(barrier, 2 + rounds + nch - 1)

    halo = pltpu.make_async_remote_copy(halo_out, halo_in, halo_send, halo_recv,
                                        device_id={"seq": right}, device_id_type=MESH)

    @pl.when(me < n - 1)
    def _():
        halo.start()

    lane = lax.broadcasted_iota(jnp.int32, (1, LANES), 1)
    lane_group = lane // modes
    lags_rev = (half - 1 - lax.broadcasted_iota(jnp.int32, (1, half), 1)).astype(f32)
    after = (lax.broadcasted_iota(jnp.int32, (half, 1), 0) + 1).astype(f32)
    own_mode = (lax.broadcasted_iota(jnp.int32, (modes, LANES), 1) % modes
                == lax.broadcasted_iota(jnp.int32, (modes, LANES), 0))

    def prepare(i, _):
        logs = decay_ref[pl.ds(pl.multiple_of(i * per, per), per), :]
        res = residue_ref[pl.ds(pl.multiple_of(i * per, per), per), :]
        pole = jnp.exp(logs)
        weight = res * jnp.sqrt(1.0 - pole * pole)
        cols, wcols = logs.T, weight.T
        rows = []
        wide_rate = jnp.zeros((modes, LANES), f32)
        wide_w = jnp.zeros((modes, LANES), f32)
        for j in range(per):
            col = jnp.broadcast_to(cols[:, j:j + 1], (modes, LANES))
            wcol = jnp.broadcast_to(wcols[:, j:j + 1], (modes, LANES))
            power = jnp.exp(col * lags_rev)
            leaving[pl.ds(pl.multiple_of(i * LANES, LANES) + j * modes, modes), :] = power.astype(bf16)
            rows.append(jnp.sum(power * wcol, axis=0, keepdims=True))
            wide_rate = jnp.where(lane_group == j, col, wide_rate)
            wide_w = jnp.where(lane_group == j, wcol, wide_w)
        hrev[pl.ds(pl.multiple_of(i * per, per), per), :] = jnp.concatenate(rows, axis=0)
        rate[:, tile_at(i)] = wide_rate
        wide_weight[:, tile_at(i)] = wide_w
        return 0

    loads[0].wait()
    loads[1].wait()
    decay_ref[...] = decay_flat[...].T
    residue_ref[...] = residue_flat[...].T
    lax.fori_loop(0, tiles, prepare, 0)
    for load in loads[2:6]:
        load.wait()

    @pl.when(me > 0)
    def _():
        halo.wait_recv()

    @pl.when(me == 0)
    def _():
        halo_in[...] = jnp.zeros_like(halo_in)

    def short(ref, which, i, slot=0):
        place = 3 * slot + which
        x = ref[:, tile_at(i)].astype(f32)
        pad[place, 8:8 + tok, :] = x
        before = halo_in[:, tile_at(i)].astype(f32)
        pad[place, 0:8, :] = pltpu.roll(before, 6 - 2 * which, 0) if which < 3 else before
        a = [taps_ref[3 * which + t:3 * which + t + 1, tile_at(i)] for t in range(3)]
        return a[0] * x + a[1] * pad[place, 7:7 + tok, :] + a[2] * pad[place, 6:6 + tok, :]

    def pick(stacked):
        out = stacked[0:modes]
        for j in range(1, per):
            out = jnp.where(lane_group == j, stacked[j * modes:(j + 1) * modes], out)
        return out

    def summarize(p):
        def body(i, _):
            pair = [2 * i, 2 * i + 1]
            values = [(short(k_ref, 1, t, u) * short(v_ref, 2, t, u)).astype(bf16) for u, t in enumerate(pair)]
            for u, t in enumerate(pair):
                mixed[:, tile_at(t)] = values[u]
                sides = jnp.concatenate([values[u][:half], values[u][half:]], axis=1)
                spread = jnp.dot(leaving[tile_at(t), :], sides, preferred_element_type=f32)
                one, two = pick(spread[:, :LANES]), pick(spread[:, LANES:])
                state = jnp.exp(rate[:, tile_at(t)] * float(half)) * one + two
                first_half[:, tile_at(t)] = one
                total[:, tile_at(t)] = state
                first_out[p, :, tile_at(t - p * part_tiles)] = state.astype(bf16)
            return 0

        lax.fori_loop(p * part_tiles // 2, (p + 1) * part_tiles // 2, body, 0)

    for p in range(PARTS):
        summarize(p)
        scan_copy(p, 0).start()

    causal = (lax.broadcasted_iota(jnp.int32, (half, LANES), 1)
              <= lax.broadcasted_iota(jnp.int32, (half, LANES), 0))

    def diagonal(state):
        fine = state.astype(bf16).astype(f32)
        return jnp.concatenate([jnp.where(lane_group == j, fine, 0.0) for j in range(per)], axis=0).astype(bf16)

    def convolve(i, _):
        values = mixed[:, tile_at(i)]
        first, second = values[:half], values[half:]
        sides = jnp.concatenate([first, second], axis=1)
        row = jnp.sum(jnp.where(own_mode, rate[:, tile_at(i)], 0.0), axis=0, keepdims=True)
        ent = jnp.exp(after * row).astype(bf16)
        entering[:, tile_at(i)] = ent
        lines = hrev[pl.ds(pl.multiple_of(i * per, per), per), :]
        left_side, right_side = [], []
        both_groups = jnp.concatenate([lane_group, lane_group], axis=1)
        for j in range(per):
            line = jnp.broadcast_to(lines[j:j + 1], (half, LANES))
            block = pltpu.roll(line, 1, 1, stride=1, stride_axis=0)
            left_side.append(jnp.where(causal, block, 0.0).astype(bf16))
            right_side.append(jnp.where(both_groups == j, sides, jnp.zeros_like(sides)))
        state = diagonal(first_half[:, tile_at(i)] * wide_weight[:, tile_at(i)])
        left_side.append(ent)
        right_side.append(jnp.concatenate([jnp.zeros_like(state), state], axis=1))
        product = jnp.dot(jnp.concatenate(left_side, axis=1), jnp.concatenate(right_side, axis=0),
                          preferred_element_type=f32)
        skip = skip_ref[:, tile_at(i)]
        conv[:half, tile_at(i)] = product[:, :LANES] + skip * first.astype(f32)
        conv[half:, tile_at(i)] = product[:, LANES:] + skip * second.astype(f32)
        q_ref[:, tile_at(i)] = short(q_ref, 0, i).astype(bf16)
        return 0

    loads[6].wait()

    carry[...] = jnp.zeros_like(carry)
    core = lax.rem(me, 2)
    weights = [max(tiles // 16, 1)] + [tiles] * (rounds - 1)
    lead = weights[0]
    bounds = [0] + [lead + (tiles - lead) * r // (rounds - 1) for r in range(rounds)]
    for r in range(rounds):
        bit = 1 << r
        last = r == rounds - 1
        upper = lax.rem(lax.div(me, bit), 2) == 1
        lax.fori_loop(bounds[r], bounds[r + 1], convolve, 0)
        block_rate = float(tok * bit)
        offset = ((lax.rem(me, bit) - core) * tok).astype(f32) if r else None

        def merge(p, i):
            local = core * half_tiles + i
            place = tile_at(p * part_tiles + local)
            theirs = (state_in[p, r, :, tile_at(i)] if r else first_in[p, :, tile_at(local)]).astype(f32)
            logs = rate[:, place]
            if r:
                inward = jnp.exp(logs * offset) * theirs
                carry[p, :, tile_at(i)] += jnp.where(upper, inward, 0.0)
            if not last:
                mine = total[:, place]
                later = jnp.where(upper, mine, theirs)
                before = jnp.where(upper, theirs, mine)
                both = jnp.exp(logs * block_rate) * before + later
                total[:, place] = both
                state_out[p, r + 1, :, tile_at(i)] = both.astype(bf16)

        def arrive(p):
            scan_copy(p, r).wait_recv()

            def body(i, _):
                merge(p, i)
                return 0

            lax.fori_loop(0, half_tiles, body, 0, unroll=4)

        for p in range(PARTS):
            if last:
                @pl.when(upper)
                def _():
                    arrive(p)

                share_copy(p).start()
            else:
                arrive(p)
                following = scan_copy(p, r + 1)
                if r + 1 == rounds - 1:
                    @pl.when(lax.rem(lax.div(me, 2 * bit), 2) == 0)
                    def _():
                        following.start()
                else:
                    following.start()

    def assemble(p):
        def body(i, _):
            for part, side in ((carry, core), (carry_in, 1 - core)):
                local = side * half_tiles + i
                place = tile_at(p * part_tiles + local)
                entry = part[p, :, tile_at(i)]
                moved = jnp.exp(rate[:, place] * float(tok)) * entry + first_in[p, :, tile_at(local)].astype(f32)
                total[:, place] = jnp.where(core == 1, moved, entry)
            return 0

        lax.fori_loop(0, half_tiles, body, 0, unroll=2)

    square[...] = jnp.zeros_like(square)

    def gated_tile(i):
        state = total[:, tile_at(i)] * wide_weight[:, tile_at(i)]
        later = state * jnp.exp(rate[:, tile_at(i)] * float(half))
        columns = []
        for s in (state, later):
            fine = s.astype(bf16).astype(f32)
            columns.append(jnp.concatenate([diagonal(fine), diagonal(s - fine)], axis=0))
        ent = entering[:, tile_at(i)]
        carried = jnp.dot(jnp.concatenate([ent, ent], axis=1), jnp.concatenate(columns, axis=1),
                          preferred_element_type=f32)
        gated = []
        for side in range(2):
            rows = slice(side * half, (side + 1) * half)
            g = q_ref[rows, tile_at(i)].astype(f32) * (conv[rows, tile_at(i)] + carried[:, side * LANES:(side + 1) * LANES])
            conv[rows, tile_at(i)] = g
            gated.append(g)
        return gated

    def gate(i, _):
        one, two = gated_tile(2 * i), gated_tile(2 * i + 1)
        for side in range(2):
            rows = slice(side * half, (side + 1) * half)
            square[rows, :] += one[side] * one[side] + two[side] * two[side]
        return 0

    for p in range(PARTS):
        share_copy(p).wait()
        assemble(p)
        lax.fori_loop(p * part_tiles // 2, (p + 1) * part_tiles // 2, gate, 0)

    sums = jnp.sum(square[...].T, axis=0, keepdims=True)
    square_out[...] = jnp.broadcast_to(sums, square_out.shape)
    copies = []
    for d in range(1, nch):
        c = pltpu.make_async_remote_copy(square_out, square_in.at[d - 1], square_send.at[d - 1], square_recv.at[d - 1],
                                         device_id={"ch": lax.rem(mych + d, nch)}, device_id_type=MESH)
        c.start()
        copies.append(c)
    for d, c in enumerate(copies):
        c.wait()
        sums = sums + square_in[d, 0:1, :]
    scale = lax.rsqrt(sums / (channels * nch) + 1e-5)
    square[...] = jnp.broadcast_to(scale, (LANES, tok)).T

    @pl.when(me < n - 1)
    def _():
        halo.wait_send()

    for p in range(PARTS):
        for r in range(rounds):
            bit = 1 << r
            copy = scan_copy(p, r)
            if r == rounds - 1:
                @pl.when(lax.rem(lax.div(me, bit), 2) == 0)
                def _():
                    copy.wait_send()
            else:
                copy.wait_send()


def normalize(gated_ref, scale_ref, gain_ref, out_hbm, out_ref, sem):
    pieces = out_ref.shape[0]
    width = out_ref.shape[2]

    def copy(j):
        return pltpu.make_async_copy(out_ref.at[j], out_hbm.at[:, j * width:(j + 1) * width], sem.at[j])

    for j in range(pieces):
        for i in range(width // LANES):
            place = slice(j * width + i * LANES, j * width + (i + 1) * LANES)
            out_ref[j, :, i * LANES:(i + 1) * LANES] = (gated_ref[:, place] * scale_ref[...] * gain_ref[:, place]).astype(bf16)
        copy(j).start()
    for j in range(pieces):
        copy(j).wait()


def on_device(n, nch, q_proj, k_proj, v_proj, short_filter, log_decay, residue, skip_bias, norm_gain):
    tok, channels = q_proj.shape
    groups, modes = log_decay.shape
    rounds = n.bit_length() - 1
    assert channels % (4 * PARTS * LANES) == 0 and n == 1 << rounds and rounds > 1 and channels == groups * modes
    vmem = pl.BlockSpec(memory_space=pltpu.VMEM)
    dma = pltpu.SemaphoreType.DMA
    part = channels // PARTS
    gated, scale = pl.pallas_call(
        functools.partial(kernel, n, nch, rounds, modes),
        out_shape=(jax.ShapeDtypeStruct((tok, channels), f32), jax.ShapeDtypeStruct((tok, LANES), f32)),
        in_specs=[pl.BlockSpec(memory_space=pltpu.HBM)] * 7,
        out_specs=(vmem, vmem),
        scratch_shapes=[
            pltpu.VMEM((tok, channels), bf16),
            pltpu.VMEM((tok, channels), bf16),
            pltpu.VMEM((tok, channels), bf16),
            pltpu.VMEM((9, channels), f32),
            pltpu.VMEM((modes, groups), f32),
            pltpu.VMEM((modes, groups), f32),
            pltpu.VMEM((1, channels), f32),
            pltpu.VMEM((3, 16, channels), bf16),
            pltpu.VMEM((groups, modes), f32),
            pltpu.VMEM((groups, modes), f32),
            pltpu.VMEM((8, channels), bf16),
            pltpu.VMEM((8, channels), bf16),
            pltpu.VMEM((6, tok + 8, LANES), f32),
            pltpu.VMEM((channels, tok // 2), bf16),
            pltpu.VMEM((groups, tok // 2), f32),
            pltpu.VMEM((tok // 2, channels), bf16),
            pltpu.VMEM((tok, channels), bf16),
            pltpu.VMEM((modes, channels), f32),
            pltpu.VMEM((modes, channels), f32),
            pltpu.VMEM((modes, channels), f32),
            pltpu.VMEM((modes, channels), f32),
            pltpu.VMEM((PARTS, modes, part // 2), f32),
            pltpu.VMEM((PARTS, modes, part // 2), f32),
            pltpu.VMEM((PARTS, modes, part), bf16),
            pltpu.VMEM((PARTS, modes, part), bf16),
            pltpu.VMEM((PARTS, rounds, modes, part // 2), bf16),
            pltpu.VMEM((PARTS, rounds, modes, part // 2), bf16),
            pltpu.VMEM((8, tok), f32),
            pltpu.VMEM((max(nch - 1, 1), 8, tok), f32),
            dma, dma, dma((PARTS, rounds)), dma((PARTS, rounds)), dma((max(nch - 1, 1),)), dma((max(nch - 1, 1),)),
            dma((7,)), dma((3,)), dma((PARTS,)), dma((PARTS,)),
        ],
        compiler_params=pltpu.CompilerParams(collective_id=0, has_side_effects=True,
                                             vmem_limit_bytes=LIMIT_A),
    )(*[pltpu.with_memory_space_constraint(x, pltpu.HBM) for x in (q_proj, k_proj, v_proj, short_filter, log_decay.T, residue.T, skip_bias.reshape(1, channels))])
    pieces = 8
    return pl.pallas_call(
        normalize,
        out_shape=jax.ShapeDtypeStruct((tok, channels), bf16),
        in_specs=[vmem, vmem, vmem],
        out_specs=pl.BlockSpec(memory_space=pltpu.HBM),
        scratch_shapes=[pltpu.VMEM((pieces, tok, channels // pieces), bf16), dma((pieces,))],
        compiler_params=pltpu.CompilerParams(vmem_limit_bytes=LIMIT_B),
    )(gated, scale, norm_gain.reshape(1, channels))


LIMIT_A = 28 * 1024 * 1024
LIMIT_B = 16 * 1024 * 1024


def solution(mesh):
    return jax.shard_map(
        functools.partial(on_device, mesh.shape["seq"], mesh.shape["ch"]),
        mesh=mesh,
        in_specs=(P("seq", "ch"), P("seq", "ch"), P("seq", "ch"), P(None, "ch"),
                  P("ch", None), P("ch", None), P("ch"), P("ch")),
        out_specs=P("seq", "ch"),
        check_vma=False,
    )
```

time: 46.8 us -> 39.2 us (0.84)
  Pallas kernels: 43.5 us -> 39 us
  local copies, waits for them, and re-layouts: 3.13 us -> 0.01 us
    pallas_call x1, Pallas kernels: 43.5 us -> 37.6 us  [on_device(): pl.pallas_call(functools.partial(kernel, n, nch, rounds, modes), out_shap...]
    unnamed x1 -> x2, local copies, waits for them, and re-layouts: 3.13 us -> 0.01 us
    pallas_call x0 -> x1, Pallas kernels: none -> 1.45 us  [on_device(): pl.pallas_call(normalize, out_shape=jax.ShapeDtypeStruct((tok, channels),...]
where the time goes in v2:
time: 39.2 us; the launch traced here: 39.1 us
  Pallas kernels  39 us (99%)
    pallas_call x1, Pallas kernels, on_device(): pl.pallas_call(functools.partial(kernel, n, nch, rounds, modes), out_shap...  37.6 us
    pallas_call x1, Pallas kernels, on_device(): pl.pallas_call(normalize, out_shape=jax.ShapeDtypeStruct((tok, channels),...  1.45 us

profile of v2, /device:TPU:0, one launch (start us, length us, event | category | flops | bytes accessed | tf_op | source)
XLA Modules:
  0.0 39.1 jit_solution(7375481362314482594)
XLA Ops:
  0.0 0.0 copy-start
  0.0 37.6 %shard_map.82 = (f32[256,4096]{1,0:T(8,128)S(1)}, f32[256,128]{1,0:T(8,128)S(1)}) custom-call(bf16[256,4096]{1,0:T(8,128)(2,1)} %q_hbm.1, bf16[256,4096]{1,0:T(8,128)(2,1)} %k_hbm.1, bf16[256,4096]{1,0:T(8,128)(2,1)} %v_hbm.1, f32[9,4096]{1,0:T(8,128)} %taps_hbm.1, f32[16,256]{1,0:T(8,128)} %bitcast.5, f32[16,256]{1,0:T(8,128)} %bitcast.6, f32[1,4096]{1,0:T(1,128)} %bitcast.7), custom_call_target="tpu_custom_call" | custom-call | tf_op jit(solution)/shard_map/pallas_call | solution.py:347
  37.6 0.0 copy-done
  37.6 1.4 %shard_map.83 = bf16[256,4096]{1,0:T(8,128)(2,1)} custom-call(f32[256,4096]{1,0:T(8,128)S(1)} %get-tuple-element.7.gated_ref, f32[256,128]{1,0:T(8,128)S(1)} %get-tuple-element.8.scale_ref, f32[1,4096]{1,0:T(1,128)S(1)} %bitcast.4), custom_call_target="tpu_custom_call" | custom-call | tf_op jit(solution)/shard_map/pallas_call | solution.py:389
Async XLA Ops:
  0.0 37.6 %copy-start = (f32[4096]{0:T(1024)S(1)}, f32[4096]{0:T(1024)}, u32[]{:S(2)}) copy-start(f32[4096]{0:T(1024)} %param.15) | copy-start | bytes 49156

commit v3 on v2

--- a/solution.py
+++ b/solution.py
@@ -10,6 +10,7 @@
 PARTS = 2
 MESH = pl.DeviceIdType.MESH
 f32 = jnp.float32
+LOG2E = 1.4426950408889634
 bf16 = jnp.bfloat16
 
 
@@ -19,7 +20,7 @@
 
 def kernel(n, nch, rounds, modes, q_hbm, k_hbm, v_hbm, taps_hbm, decay_hbm, residue_hbm, skip_hbm,
            conv, square, q_ref, k_ref, v_ref, taps_ref, decay_flat, residue_flat, skip_ref,
-           tails, decay_ref, residue_ref, halo_out, halo_in, pad, leaving, hrev, entering, mixed, rate, wide_weight,
+           tails, halo_out, halo_in, pad, leaving, hrev, entering, mixed, rate, wide_weight,
            total, first_half, carry, carry_in, first_out, first_in, state_out, state_in, square_out, square_in,
            halo_send, halo_recv, state_send, state_recv, square_send, square_recv, load_sem, tail_sem, carry_send, carry_recv):
     tok, channels = q_ref.shape
@@ -82,33 +83,37 @@
     own_mode = (lax.broadcasted_iota(jnp.int32, (modes, LANES), 1) % modes
                 == lax.broadcasted_iota(jnp.int32, (modes, LANES), 0))
 
+    group_row = lax.broadcasted_iota(jnp.int32, (per, LANES), 0)
+    blocks = LANES // per
+
     def prepare(i, _):
-        logs = decay_ref[pl.ds(pl.multiple_of(i * per, per), per), :]
-        res = residue_ref[pl.ds(pl.multiple_of(i * per, per), per), :]
-        pole = jnp.exp(logs)
-        weight = res * jnp.sqrt(1.0 - pole * pole)
-        cols, wcols = logs.T, weight.T
-        rows = []
-        wide_rate = jnp.zeros((modes, LANES), f32)
-        wide_w = jnp.zeros((modes, LANES), f32)
-        for j in range(per):
-            col = jnp.broadcast_to(cols[:, j:j + 1], (modes, LANES))
-            wcol = jnp.broadcast_to(wcols[:, j:j + 1], (modes, LANES))
-            power = jnp.exp(col * lags_rev)
-            leaving[pl.ds(pl.multiple_of(i * LANES, LANES) + j * modes, modes), :] = power.astype(bf16)
-            rows.append(jnp.sum(power * wcol, axis=0, keepdims=True))
-            wide_rate = jnp.where(lane_group == j, col, wide_rate)
-            wide_w = jnp.where(lane_group == j, wcol, wide_w)
-        hrev[pl.ds(pl.multiple_of(i * per, per), per), :] = jnp.concatenate(rows, axis=0)
+        block = tile_at(lax.div(i, blocks))
+        index = jnp.broadcast_to(per * lax.rem(i, blocks) + lane_group, (modes, LANES))
+        wide_rate = jnp.take_along_axis(decay_flat[:, block], index, axis=1)
+        wide_w = jnp.take_along_axis(residue_flat[:, block], index, axis=1)
         rate[:, tile_at(i)] = wide_rate
         wide_weight[:, tile_at(i)] = wide_w
+        powers = []
+        for j in range(per):
+            col = wide_rate[:, j * modes:j * modes + 1]
+            powers.append(jnp.exp2(col * lags_rev).astype(bf16))
+        powers = jnp.concatenate(powers, axis=0)
+        leaving[tile_at(i), :] = powers
+        row = jnp.sum(jnp.where(own_mode, wide_rate, 0.0), axis=0, keepdims=True)
+        wrow = jnp.sum(jnp.where(own_mode, wide_w, 0.0), axis=0, keepdims=True)
+        spread_w = jnp.where(group_row == lane_group, wrow, 0.0)
+        coarse = spread_w.astype(bf16).astype(f32)
+        both = jnp.dot(jnp.concatenate([coarse, spread_w - coarse], axis=0).astype(bf16), powers, preferred_element_type=f32)
+        hrev[pl.ds(pl.multiple_of(i * per, per), per), :] = both[:per] + both[per:]
+        entering[:, tile_at(i)] = jnp.exp2(after * row).astype(bf16)
         return 0
 
     loads[0].wait()
     loads[1].wait()
-    decay_ref[...] = decay_flat[...].T
-    residue_ref[...] = residue_flat[...].T
-    lax.fori_loop(0, tiles, prepare, 0)
+    pole = jnp.exp(decay_flat[...])
+    residue_flat[...] = residue_flat[...] * jnp.sqrt(1.0 - pole * pole)
+    decay_flat[...] = decay_flat[...] * LOG2E
+    lax.fori_loop(0, tiles, prepare, 0, unroll=UP)
     for load in loads[2:6]:
         load.wait()
 
@@ -144,7 +149,7 @@
                 sides = jnp.concatenate([values[u][:half], values[u][half:]], axis=1)
                 spread = jnp.dot(leaving[tile_at(t), :], sides, preferred_element_type=f32)
                 one, two = pick(spread[:, :LANES]), pick(spread[:, LANES:])
-                state = jnp.exp(rate[:, tile_at(t)] * float(half)) * one + two
+                state = jnp.exp2(rate[:, tile_at(t)] * float(half)) * one + two
                 first_half[:, tile_at(t)] = one
                 total[:, tile_at(t)] = state
                 first_out[p, :, tile_at(t - p * part_tiles)] = state.astype(bf16)
@@ -167,9 +172,7 @@
         values = mixed[:, tile_at(i)]
         first, second = values[:half], values[half:]
         sides = jnp.concatenate([first, second], axis=1)
-        row = jnp.sum(jnp.where(own_mode, rate[:, tile_at(i)], 0.0), axis=0, keepdims=True)
-        ent = jnp.exp(after * row).astype(bf16)
-        entering[:, tile_at(i)] = ent
+        ent = entering[:, tile_at(i)]
         lines = hrev[pl.ds(pl.multiple_of(i * per, per), per), :]
         left_side, right_side = [], []
         both_groups = jnp.concatenate([lane_group, lane_group], axis=1)
@@ -210,13 +213,13 @@
             theirs = (state_in[p, r, :, tile_at(i)] if r else first_in[p, :, tile_at(local)]).astype(f32)
             logs = rate[:, place]
             if r:
-                inward = jnp.exp(logs * offset) * theirs
+                inward = jnp.exp2(logs * offset) * theirs
                 carry[p, :, tile_at(i)] += jnp.where(upper, inward, 0.0)
             if not last:
                 mine = total[:, place]
                 later = jnp.where(upper, mine, theirs)
                 before = jnp.where(upper, theirs, mine)
-                both = jnp.exp(logs * block_rate) * before + later
+                both = jnp.exp2(logs * block_rate) * before + later
                 total[:, place] = both
                 state_out[p, r + 1, :, tile_at(i)] = both.astype(bf16)
 
@@ -252,7 +255,7 @@
                 local = side * half_tiles + i
                 place = tile_at(p * part_tiles + local)
                 entry = part[p, :, tile_at(i)]
-                moved = jnp.exp(rate[:, place] * float(tok)) * entry + first_in[p, :, tile_at(local)].astype(f32)
+                moved = jnp.exp2(rate[:, place] * float(tok)) * entry + first_in[p, :, tile_at(local)].astype(f32)
                 total[:, place] = jnp.where(core == 1, moved, entry)
             return 0
 
@@ -262,7 +265,7 @@
 
     def gated_tile(i):
         state = total[:, tile_at(i)] * wide_weight[:, tile_at(i)]
-        later = state * jnp.exp(rate[:, tile_at(i)] * float(half))
+        later = state * jnp.exp2(rate[:, tile_at(i)] * float(half))
         columns = []
         for s in (state, later):
             fine = s.astype(bf16).astype(f32)
@@ -358,8 +361,6 @@
             pltpu.VMEM((modes, groups), f32),
             pltpu.VMEM((1, channels), f32),
             pltpu.VMEM((3, 16, channels), bf16),
-            pltpu.VMEM((groups, modes), f32),
-            pltpu.VMEM((groups, modes), f32),
             pltpu.VMEM((8, channels), bf16),
             pltpu.VMEM((8, channels), bf16),
             pltpu.VMEM((6, tok + 8, LANES), f32),
@@ -396,6 +397,7 @@
     )(gated, scale, norm_gain.reshape(1, channels))
 
 
+UP = 8
 LIMIT_A = 28 * 1024 * 1024
 LIMIT_B = 16 * 1024 * 1024
 

time: 39.2 us -> 34.8 us (0.89)
  Pallas kernels: 39 us -> 34.6 us
    pallas_call x1, Pallas kernels: 37.6 us -> 33.2 us  [on_device(): pl.pallas_call(functools.partial(kernel, n, nch, rounds, modes), out_shap...]
where the time goes in v3:
time: 34.8 us; the launch traced here: 34.7 us
  Pallas kernels  34.6 us (99%)
    pallas_call x1, Pallas kernels, on_device(): pl.pallas_call(functools.partial(kernel, n, nch, rounds, modes), out_shap...  33.2 us
    pallas_call x1, Pallas kernels, on_device(): pl.pallas_call(normalize, out_shape=jax.ShapeDtypeStruct((tok, channels),...  1.45 us

profile of v3, /device:TPU:0, one launch (start us, length us, event | category | flops | bytes accessed | tf_op | source)
XLA Modules:
  0.0 34.7 jit_solution(5091124123974185973)
XLA Ops:
  0.0 0.0 copy-start
  0.0 33.2 %shard_map.82 = (f32[256,4096]{1,0:T(8,128)S(1)}, f32[256,128]{1,0:T(8,128)S(1)}) custom-call(bf16[256,4096]{1,0:T(8,128)(2,1)} %q_hbm.1, bf16[256,4096]{1,0:T(8,128)(2,1)} %k_hbm.1, bf16[256,4096]{1,0:T(8,128)(2,1)} %v_hbm.1, f32[9,4096]{1,0:T(8,128)} %taps_hbm.1, f32[16,256]{1,0:T(8,128)} %bitcast.5, f32[16,256]{1,0:T(8,128)} %bitcast.6, f32[1,4096]{1,0:T(1,128)} %bitcast.7), custom_call_target="tpu_custom_call" | custom-call | tf_op jit(solution)/shard_map/pallas_call | solution.py:350
  33.2 0.0 copy-done
  33.2 1.4 %shard_map.83 = bf16[256,4096]{1,0:T(8,128)(2,1)} custom-call(f32[256,4096]{1,0:T(8,128)S(1)} %get-tuple-element.7.gated_ref, f32[256,128]{1,0:T(8,128)S(1)} %get-tuple-element.8.scale_ref, f32[1,4096]{1,0:T(1,128)S(1)} %bitcast.4), custom_call_target="tpu_custom_call" | custom-call | tf_op jit(solution)/shard_map/pallas_call | solution.py:390
Async XLA Ops:
  0.0 33.2 %copy-start = (f32[4096]{0:T(1024)S(1)}, f32[4096]{0:T(1024)}, u32[]{:S(2)}) copy-start(f32[4096]{0:T(1024)} %param.15) | copy-start | bytes 49156

commit v4 on v3

--- a/solution.py
+++ b/solution.py
@@ -7,7 +7,7 @@
 from jax.sharding import PartitionSpec as P
 
 LANES = 128
-PARTS = 2
+MOST_PARTS = 4
 MESH = pl.DeviceIdType.MESH
 f32 = jnp.float32
 LOG2E = 1.4426950408889634
@@ -26,6 +26,7 @@
     tok, channels = q_ref.shape
     half = tok // 2
     tiles = channels // LANES
+    PARTS = state_send.shape[0]
     part_tiles = tiles // PARTS
     half_tiles = part_tiles // 2
     per = LANES // modes
@@ -142,7 +143,7 @@
 
     def summarize(p):
         def body(i, _):
-            pair = [2 * i, 2 * i + 1]
+            pair = [SW * i + u for u in range(SW)]
             values = [(short(k_ref, 1, t, u) * short(v_ref, 2, t, u)).astype(bf16) for u, t in enumerate(pair)]
             for u, t in enumerate(pair):
                 mixed[:, tile_at(t)] = values[u]
@@ -155,7 +156,7 @@
                 first_out[p, :, tile_at(t - p * part_tiles)] = state.astype(bf16)
             return 0
 
-        lax.fori_loop(p * part_tiles // 2, (p + 1) * part_tiles // 2, body, 0)
+        lax.fori_loop(p * part_tiles // SW, (p + 1) * part_tiles // SW, body, 0, unroll=SU)
 
     for p in range(PARTS):
         summarize(p)
@@ -168,7 +169,7 @@
         fine = state.astype(bf16).astype(f32)
         return jnp.concatenate([jnp.where(lane_group == j, fine, 0.0) for j in range(per)], axis=0).astype(bf16)
 
-    def convolve(i, _):
+    def convolve_tile(i, slot):
         values = mixed[:, tile_at(i)]
         first, second = values[:half], values[half:]
         sides = jnp.concatenate([first, second], axis=1)
@@ -189,21 +190,26 @@
         skip = skip_ref[:, tile_at(i)]
         conv[:half, tile_at(i)] = product[:, :LANES] + skip * first.astype(f32)
         conv[half:, tile_at(i)] = product[:, LANES:] + skip * second.astype(f32)
-        q_ref[:, tile_at(i)] = short(q_ref, 0, i).astype(bf16)
+        q_ref[:, tile_at(i)] = short(q_ref, 0, i, slot).astype(bf16)
+
+    def convolve(i, _):
+        for u in range(CW):
+            convolve_tile(CW * i + u, u)
         return 0
 
     loads[6].wait()
 
     carry[...] = jnp.zeros_like(carry)
     core = lax.rem(me, 2)
-    weights = [max(tiles // 16, 1)] + [tiles] * (rounds - 1)
-    lead = weights[0]
-    bounds = [0] + [lead + (tiles - lead) * r // (rounds - 1) for r in range(rounds)]
+    steps = tiles // CW
+    lead = min(LEAD, steps)
+    shares = [2] * (rounds - 2) + [LASTW]
+    bounds = [0] + [lead + (steps - lead) * sum(shares[:r]) // sum(shares) for r in range(rounds)]
     for r in range(rounds):
         bit = 1 << r
         last = r == rounds - 1
         upper = lax.rem(lax.div(me, bit), 2) == 1
-        lax.fori_loop(bounds[r], bounds[r + 1], convolve, 0)
+        lax.fori_loop(bounds[r], bounds[r + 1], convolve, 0, unroll=CU)
         block_rate = float(tok * bit)
         offset = ((lax.rem(me, bit) - core) * tok).astype(f32) if r else None
 
@@ -282,16 +288,16 @@
         return gated
 
     def gate(i, _):
-        one, two = gated_tile(2 * i), gated_tile(2 * i + 1)
+        done = [gated_tile(GW * i + u) for u in range(GW)]
         for side in range(2):
             rows = slice(side * half, (side + 1) * half)
-            square[rows, :] += one[side] * one[side] + two[side] * two[side]
+            square[rows, :] += sum(g[side] * g[side] for g in done)
         return 0
 
     for p in range(PARTS):
         share_copy(p).wait()
         assemble(p)
-        lax.fori_loop(p * part_tiles // 2, (p + 1) * part_tiles // 2, gate, 0)
+        lax.fori_loop(p * part_tiles // GW, (p + 1) * part_tiles // GW, gate, 0, unroll=GU)
 
     sums = jnp.sum(square[...].T, axis=0, keepdims=True)
     square_out[...] = jnp.broadcast_to(sums, square_out.shape)
@@ -343,9 +349,10 @@
     tok, channels = q_proj.shape
     groups, modes = log_decay.shape
     rounds = n.bit_length() - 1
-    assert channels % (4 * PARTS * LANES) == 0 and n == 1 << rounds and rounds > 1 and channels == groups * modes
+    assert channels % (4 * LANES) == 0 and n == 1 << rounds and rounds > 1 and channels == groups * modes
     vmem = pl.BlockSpec(memory_space=pltpu.VMEM)
     dma = pltpu.SemaphoreType.DMA
+    PARTS = min(MOST_PARTS, channels // (4 * LANES))
     part = channels // PARTS
     gated, scale = pl.pallas_call(
         functools.partial(kernel, n, nch, rounds, modes),
@@ -363,7 +370,7 @@
             pltpu.VMEM((3, 16, channels), bf16),
             pltpu.VMEM((8, channels), bf16),
             pltpu.VMEM((8, channels), bf16),
-            pltpu.VMEM((6, tok + 8, LANES), f32),
+            pltpu.VMEM((3 * max(SW, CW), tok + 8, LANES), f32),
             pltpu.VMEM((channels, tok // 2), bf16),
             pltpu.VMEM((groups, tok // 2), f32),
             pltpu.VMEM((tok // 2, channels), bf16),
@@ -398,6 +405,7 @@
 
 
 UP = 8
+SW, SU, CW, CU, GW, GU, LEAD, LASTW = 2, 4, 2, 2, 2, 4, 1, 2
 LIMIT_A = 28 * 1024 * 1024
 LIMIT_B = 16 * 1024 * 1024
 

time: 34.8 us -> 27.2 us (0.78)
  Pallas kernels: 34.6 us -> 27 us
    pallas_call x1, Pallas kernels: 33.2 us -> 25.6 us  [on_device(): pl.pallas_call(functools.partial(kernel, n, nch, rounds, modes), out_shap...]
where the time goes in v4:
time: 27.2 us; the launch traced here: 27 us
  Pallas kernels  27 us (99%)
    pallas_call x1, Pallas kernels, on_device(): pl.pallas_call(functools.partial(kernel, n, nch, rounds, modes), out_shap...  25.6 us
    pallas_call x1, Pallas kernels, on_device(): pl.pallas_call(normalize, out_shape=jax.ShapeDtypeStruct((tok, channels),...  1.45 us

profile of v4, /device:TPU:0, one launch (start us, length us, event | category | flops | bytes accessed | tf_op | source)
XLA Modules:
  0.0 27.0 jit_solution(17777756040835127931)
XLA Ops:
  0.0 0.0 copy-start
  0.0 25.6 %shard_map.82 = (f32[256,4096]{1,0:T(8,128)S(1)}, f32[256,128]{1,0:T(8,128)S(1)}) custom-call(bf16[256,4096]{1,0:T(8,128)(2,1)} %q_hbm.1, bf16[256,4096]{1,0:T(8,128)(2,1)} %k_hbm.1, bf16[256,4096]{1,0:T(8,128)(2,1)} %v_hbm.1, f32[9,4096]{1,0:T(8,128)} %taps_hbm.1, f32[16,256]{1,0:T(8,128)} %bitcast.5, f32[16,256]{1,0:T(8,128)} %bitcast.6, f32[1,4096]{1,0:T(1,128)} %bitcast.7), custom_call_target="tpu_custom_call" | custom-call | tf_op jit(solution)/shard_map/pallas_call | solution.py:357
  25.6 0.0 copy-done
  25.6 1.4 %shard_map.83 = bf16[256,4096]{1,0:T(8,128)(2,1)} custom-call(f32[256,4096]{1,0:T(8,128)S(1)} %get-tuple-element.7.gated_ref, f32[256,128]{1,0:T(8,128)S(1)} %get-tuple-element.8.scale_ref, f32[1,4096]{1,0:T(1,128)S(1)} %bitcast.4), custom_call_target="tpu_custom_call" | custom-call | tf_op jit(solution)/shard_map/pallas_call | solution.py:397
Async XLA Ops:
  0.0 25.6 %copy-start = (f32[4096]{0:T(1024)S(1)}, f32[4096]{0:T(1024)}, u32[]{:S(2)}) copy-start(f32[4096]{0:T(1024)} %param.15) | copy-start | bytes 49156

commit v5 on v4

--- a/solution.py
+++ b/solution.py
@@ -20,7 +20,7 @@
 
 def kernel(n, nch, rounds, modes, q_hbm, k_hbm, v_hbm, taps_hbm, decay_hbm, residue_hbm, skip_hbm,
            conv, square, q_ref, k_ref, v_ref, taps_ref, decay_flat, residue_flat, skip_ref,
-           tails, halo_out, halo_in, pad, leaving, hrev, entering, mixed, rate, wide_weight,
+           tails, halo_out, halo_in, pad, leaving, hrev, entering, mixed, q_short, rate, wide_weight,
            total, first_half, carry, carry_in, first_out, first_in, state_out, state_in, square_out, square_in,
            halo_send, halo_recv, state_send, state_recv, square_send, square_recv, load_sem, tail_sem, carry_send, carry_recv):
     tok, channels = q_ref.shape
@@ -32,7 +32,7 @@
     per = LANES // modes
     me = lax.axis_index("seq")
     mych = lax.axis_index("ch")
-    right, left = lax.rem(me + 1, n), lax.rem(me + n - 1, n)
+    right = lax.rem(me + 1, n)
 
     def partner(bit):
         return me + bit * (1 - 2 * lax.rem(lax.div(me, bit), 2))
@@ -54,10 +54,23 @@
     for load in tail_loads + loads:
         load.start()
     barrier = pltpu.get_barrier_semaphore()
-    for other in [right, left] + [partner(1 << r) for r in range(rounds)]:
-        pl.semaphore_signal(barrier, inc=1, device_id={"seq": other}, device_id_type=MESH)
+    top = n // 2
+
+    def ready(device):
+        pl.semaphore_signal(barrier, inc=1, device_id=device, device_id_type=MESH)
+
+    @pl.when(me >= top)
+    def _():
+        ready({"seq": me - top})
+
+    @pl.when(me > 0)
+    def _():
+        ready({"seq": me - 1})
+
+    for r in range(rounds - 1):
+        ready({"seq": partner(1 << r)})
     for d in range(1, nch):
-        pl.semaphore_signal(barrier, inc=1, device_id={"ch": lax.rem(mych + d, nch)}, device_id_type=MESH)
+        ready({"ch": lax.rem(mych + d, nch)})
 
     for load in tail_loads:
         load.wait()
@@ -68,7 +81,8 @@
         return 0
 
     lax.fori_loop(0, tiles, make_halo, 0, unroll=4)
-    pl.semaphore_wait(barrier, 2 + rounds + nch - 1)
+    fixed = rounds - 1 + nch - 1
+    pl.semaphore_wait(barrier, fixed + (me < n - 1).astype(jnp.int32) + (me < top).astype(jnp.int32))
 
     halo = pltpu.make_async_remote_copy(halo_out, halo_in, halo_send, halo_recv,
                                         device_id={"seq": right}, device_id_type=MESH)
@@ -106,7 +120,7 @@
         coarse = spread_w.astype(bf16).astype(f32)
         both = jnp.dot(jnp.concatenate([coarse, spread_w - coarse], axis=0).astype(bf16), powers, preferred_element_type=f32)
         hrev[pl.ds(pl.multiple_of(i * per, per), per), :] = both[:per] + both[per:]
-        entering[:, tile_at(i)] = jnp.exp2(after * row).astype(bf16)
+        entering[i] = jnp.exp2(after * row).astype(bf16)
         return 0
 
     loads[0].wait()
@@ -146,7 +160,7 @@
             pair = [SW * i + u for u in range(SW)]
             values = [(short(k_ref, 1, t, u) * short(v_ref, 2, t, u)).astype(bf16) for u, t in enumerate(pair)]
             for u, t in enumerate(pair):
-                mixed[:, tile_at(t)] = values[u]
+                mixed[t] = values[u]
                 sides = jnp.concatenate([values[u][:half], values[u][half:]], axis=1)
                 spread = jnp.dot(leaving[tile_at(t), :], sides, preferred_element_type=f32)
                 one, two = pick(spread[:, :LANES]), pick(spread[:, LANES:])
@@ -158,10 +172,6 @@
 
         lax.fori_loop(p * part_tiles // SW, (p + 1) * part_tiles // SW, body, 0, unroll=SU)
 
-    for p in range(PARTS):
-        summarize(p)
-        scan_copy(p, 0).start()
-
     causal = (lax.broadcasted_iota(jnp.int32, (half, LANES), 1)
               <= lax.broadcasted_iota(jnp.int32, (half, LANES), 0))
 
@@ -170,10 +180,10 @@
         return jnp.concatenate([jnp.where(lane_group == j, fine, 0.0) for j in range(per)], axis=0).astype(bf16)
 
     def convolve_tile(i, slot):
-        values = mixed[:, tile_at(i)]
+        values = mixed[i]
         first, second = values[:half], values[half:]
         sides = jnp.concatenate([first, second], axis=1)
-        ent = entering[:, tile_at(i)]
+        ent = entering[i]
         lines = hrev[pl.ds(pl.multiple_of(i * per, per), per), :]
         left_side, right_side = [], []
         both_groups = jnp.concatenate([lane_group, lane_group], axis=1)
@@ -190,30 +200,24 @@
         skip = skip_ref[:, tile_at(i)]
         conv[:half, tile_at(i)] = product[:, :LANES] + skip * first.astype(f32)
         conv[half:, tile_at(i)] = product[:, LANES:] + skip * second.astype(f32)
-        q_ref[:, tile_at(i)] = short(q_ref, 0, i, slot).astype(bf16)
+        q_short[i] = short(q_ref, 0, i, slot).astype(bf16)
 
     def convolve(i, _):
         for u in range(CW):
             convolve_tile(CW * i + u, u)
         return 0
 
-    loads[6].wait()
-
     carry[...] = jnp.zeros_like(carry)
     core = lax.rem(me, 2)
-    steps = tiles // CW
-    lead = min(LEAD, steps)
-    shares = [2] * (rounds - 2) + [LASTW]
-    bounds = [0] + [lead + (steps - lead) * sum(shares[:r]) // sum(shares) for r in range(rounds)]
-    for r in range(rounds):
+
+    def arrive(p, r):
         bit = 1 << r
         last = r == rounds - 1
         upper = lax.rem(lax.div(me, bit), 2) == 1
-        lax.fori_loop(bounds[r], bounds[r + 1], convolve, 0, unroll=CU)
         block_rate = float(tok * bit)
         offset = ((lax.rem(me, bit) - core) * tok).astype(f32) if r else None
 
-        def merge(p, i):
+        def merge(i, _):
             local = core * half_tiles + i
             place = tile_at(p * part_tiles + local)
             theirs = (state_in[p, r, :, tile_at(i)] if r else first_in[p, :, tile_at(local)]).astype(f32)
@@ -228,32 +232,40 @@
                 both = jnp.exp2(logs * block_rate) * before + later
                 total[:, place] = both
                 state_out[p, r + 1, :, tile_at(i)] = both.astype(bf16)
-
-        def arrive(p):
+            return 0
+
+        def receive():
             scan_copy(p, r).wait_recv()
-
-            def body(i, _):
-                merge(p, i)
-                return 0
-
-            lax.fori_loop(0, half_tiles, body, 0, unroll=4)
-
-        for p in range(PARTS):
-            if last:
-                @pl.when(upper)
-                def _():
-                    arrive(p)
-
-                share_copy(p).start()
+            lax.fori_loop(0, half_tiles, merge, 0, unroll=4)
+
+        if last:
+            pl.when(upper)(receive)
+            share_copy(p).start()
+        else:
+            receive()
+            following = scan_copy(p, r + 1)
+            if r + 1 == rounds - 1:
+                pl.when(lax.rem(lax.div(me, 2 * bit), 2) == 0)(following.start)
             else:
-                arrive(p)
-                following = scan_copy(p, r + 1)
-                if r + 1 == rounds - 1:
-                    @pl.when(lax.rem(lax.div(me, 2 * bit), 2) == 0)
-                    def _():
-                        following.start()
-                else:
-                    following.start()
+                following.start()
+
+    for p in range(PARTS):
+        summarize(p)
+        scan_copy(p, 0).start()
+        if p:
+            arrive(p - 1, 0)
+
+    loads[6].wait()
+    events = [(PARTS - 1, 0)] + [(p, r) for r in range(1, rounds) for p in range(PARTS)]
+    shares = [LEAD] + [FIRST if p == 0 else THEN for r in range(1, rounds) for p in range(PARTS)]
+    steps = tiles // CW
+    done = 0
+    for k, (p, r) in enumerate(events):
+        end = (steps * sum(shares[:k + 1]) + sum(shares) // 2) // sum(shares)
+        if end > done:
+            lax.fori_loop(done, end, convolve, 0, unroll=CU)
+        done = end
+        arrive(p, r)
 
     def assemble(p):
         def body(i, _):
@@ -276,13 +288,13 @@
         for s in (state, later):
             fine = s.astype(bf16).astype(f32)
             columns.append(jnp.concatenate([diagonal(fine), diagonal(s - fine)], axis=0))
-        ent = entering[:, tile_at(i)]
+        ent = entering[i]
         carried = jnp.dot(jnp.concatenate([ent, ent], axis=1), jnp.concatenate(columns, axis=1),
                           preferred_element_type=f32)
         gated = []
         for side in range(2):
             rows = slice(side * half, (side + 1) * half)
-            g = q_ref[rows, tile_at(i)].astype(f32) * (conv[rows, tile_at(i)] + carried[:, side * LANES:(side + 1) * LANES])
+            g = q_short[i, rows, :].astype(f32) * (conv[rows, tile_at(i)] + carried[:, side * LANES:(side + 1) * LANES])
             conv[rows, tile_at(i)] = g
             gated.append(g)
         return gated
@@ -373,8 +385,9 @@
             pltpu.VMEM((3 * max(SW, CW), tok + 8, LANES), f32),
             pltpu.VMEM((channels, tok // 2), bf16),
             pltpu.VMEM((groups, tok // 2), f32),
-            pltpu.VMEM((tok // 2, channels), bf16),
-            pltpu.VMEM((tok, channels), bf16),
+            pltpu.VMEM((channels // LANES, tok // 2, LANES), bf16),
+            pltpu.VMEM((channels // LANES, tok, LANES), bf16),
+            pltpu.VMEM((channels // LANES, tok, LANES), bf16),
             pltpu.VMEM((modes, channels), f32),
             pltpu.VMEM((modes, channels), f32),
             pltpu.VMEM((modes, channels), f32),
@@ -405,7 +418,7 @@
 
 
 UP = 8
-SW, SU, CW, CU, GW, GU, LEAD, LASTW = 2, 4, 2, 2, 2, 4, 1, 2
+SW, SU, CW, CU, GW, GU, LEAD, FIRST, THEN = 2, 4, 2, 2, 2, 4, 2, 5, 2
 LIMIT_A = 28 * 1024 * 1024
 LIMIT_B = 16 * 1024 * 1024
 

time: 27.2 us -> 26.2 us (0.963)
  Pallas kernels: 27 us -> 26 us
    pallas_call x1, Pallas kernels: 25.6 us -> 24.6 us  [on_device(): pl.pallas_call(functools.partial(kernel, n, nch, rounds, modes), out_shap...]
where the time goes in v5:
time: 26.2 us; the launch traced here: 26 us
  Pallas kernels  26 us (99%)
    pallas_call x1, Pallas kernels, on_device(): pl.pallas_call(functools.partial(kernel, n, nch, rounds, modes), out_shap...  24.6 us
    pallas_call x1, Pallas kernels, on_device(): pl.pallas_call(normalize, out_shape=jax.ShapeDtypeStruct((tok, channels),...  1.45 us

profile of v5, /device:TPU:0, one launch (start us, length us, event | category | flops | bytes accessed | tf_op | source)
XLA Modules:
  0.0 26.0 jit_solution(3267519597358412341)
XLA Ops:
  0.0 0.0 copy-start
  0.0 24.6 %shard_map.82 = (f32[256,4096]{1,0:T(8,128)S(1)}, f32[256,128]{1,0:T(8,128)S(1)}) custom-call(bf16[256,4096]{1,0:T(8,128)(2,1)} %q_hbm.1, bf16[256,4096]{1,0:T(8,128)(2,1)} %k_hbm.1, bf16[256,4096]{1,0:T(8,128)(2,1)} %v_hbm.1, f32[9,4096]{1,0:T(8,128)} %taps_hbm.1, f32[16,256]{1,0:T(8,128)} %bitcast.5, f32[16,256]{1,0:T(8,128)} %bitcast.6, f32[1,4096]{1,0:T(1,128)} %bitcast.7), custom_call_target="tpu_custom_call" | custom-call | tf_op jit(solution)/shard_map/pallas_call | solution.py:369
  24.6 0.0 copy-done
  24.6 1.4 %shard_map.83 = bf16[256,4096]{1,0:T(8,128)(2,1)} custom-call(f32[256,4096]{1,0:T(8,128)S(1)} %get-tuple-element.7.gated_ref, f32[256,128]{1,0:T(8,128)S(1)} %get-tuple-element.8.scale_ref, f32[1,4096]{1,0:T(1,128)S(1)} %bitcast.4), custom_call_target="tpu_custom_call" | custom-call | tf_op jit(solution)/shard_map/pallas_call | solution.py:410
Async XLA Ops:
  0.0 24.6 %copy-start = (f32[4096]{0:T(1024)S(1)}, f32[4096]{0:T(1024)}, u32[]{:S(2)}) copy-start(f32[4096]{0:T(1024)} %param.15) | copy-start | bytes 49156

commit v6 on v5

--- a/solution.py
+++ b/solution.py
@@ -193,13 +193,12 @@
             left_side.append(jnp.where(causal, block, 0.0).astype(bf16))
             right_side.append(jnp.where(both_groups == j, sides, jnp.zeros_like(sides)))
         state = diagonal(first_half[:, tile_at(i)] * wide_weight[:, tile_at(i)])
-        left_side.append(ent)
-        right_side.append(jnp.concatenate([jnp.zeros_like(state), state], axis=1))
         product = jnp.dot(jnp.concatenate(left_side, axis=1), jnp.concatenate(right_side, axis=0),
                           preferred_element_type=f32)
+        inner = jnp.dot(ent, state, preferred_element_type=f32)
         skip = skip_ref[:, tile_at(i)]
         conv[:half, tile_at(i)] = product[:, :LANES] + skip * first.astype(f32)
-        conv[half:, tile_at(i)] = product[:, LANES:] + skip * second.astype(f32)
+        conv[half:, tile_at(i)] = product[:, LANES:] + inner + skip * second.astype(f32)
         q_short[i] = short(q_ref, 0, i, slot).astype(bf16)
 
     def convolve(i, _):
@@ -284,12 +283,9 @@
     def gated_tile(i):
         state = total[:, tile_at(i)] * wide_weight[:, tile_at(i)]
         later = state * jnp.exp2(rate[:, tile_at(i)] * float(half))
-        columns = []
-        for s in (state, later):
-            fine = s.astype(bf16).astype(f32)
-            columns.append(jnp.concatenate([diagonal(fine), diagonal(s - fine)], axis=0))
+        columns = [diagonal(state), diagonal(later)]
         ent = entering[i]
-        carried = jnp.dot(jnp.concatenate([ent, ent], axis=1), jnp.concatenate(columns, axis=1),
+        carried = jnp.dot(ent, jnp.concatenate(columns, axis=1),
                           preferred_element_type=f32)
         gated = []
         for side in range(2):
@@ -418,7 +414,7 @@
 
 
 UP = 8
-SW, SU, CW, CU, GW, GU, LEAD, FIRST, THEN = 2, 4, 2, 2, 2, 4, 2, 5, 2
+SW, SU, CW, CU, GW, GU, LEAD, FIRST, THEN = 2, 4, 2, 2, 2, 4, 2, 6, 1
 LIMIT_A = 28 * 1024 * 1024
 LIMIT_B = 16 * 1024 * 1024
 

time: 26.2 us -> 26 us (level)
  no operation moved by 1% of the time
where the time goes in v6:
time: 26 us; the launch traced here: 25.9 us
  Pallas kernels  25.9 us (100%)
    pallas_call x1, Pallas kernels, on_device(): pl.pallas_call(functools.partial(kernel, n, nch, rounds, modes), out_shap...  24.4 us
    pallas_call x1, Pallas kernels, on_device(): pl.pallas_call(normalize, out_shape=jax.ShapeDtypeStruct((tok, channels),...  1.45 us

profile of v6, /device:TPU:0, one launch (start us, length us, event | category | flops | bytes accessed | tf_op | source)
XLA Modules:
  0.0 25.9 jit_solution(17753930117677936402)
XLA Ops:
  0.0 0.0 copy-start
  0.0 24.4 %shard_map.82 = (f32[256,4096]{1,0:T(8,128)S(1)}, f32[256,128]{1,0:T(8,128)S(1)}) custom-call(bf16[256,4096]{1,0:T(8,128)(2,1)} %q_hbm.1, bf16[256,4096]{1,0:T(8,128)(2,1)} %k_hbm.1, bf16[256,4096]{1,0:T(8,128)(2,1)} %v_hbm.1, f32[9,4096]{1,0:T(8,128)} %taps_hbm.1, f32[16,256]{1,0:T(8,128)} %bitcast.5, f32[16,256]{1,0:T(8,128)} %bitcast.6, f32[1,4096]{1,0:T(1,128)} %bitcast.7), custom_call_target="tpu_custom_call" | custom-call | tf_op jit(solution)/shard_map/pallas_call | solution.py:365
  24.4 0.0 copy-done
  24.4 1.4 %shard_map.83 = bf16[256,4096]{1,0:T(8,128)(2,1)} custom-call(f32[256,4096]{1,0:T(8,128)S(1)} %get-tuple-element.7.gated_ref, f32[256,128]{1,0:T(8,128)S(1)} %get-tuple-element.8.scale_ref, f32[1,4096]{1,0:T(1,128)S(1)} %bitcast.4), custom_call_target="tpu_custom_call" | custom-call | tf_op jit(solution)/shard_map/pallas_call | solution.py:406
Async XLA Ops:
  0.0 24.4 %copy-start = (f32[4096]{0:T(1024)S(1)}, f32[4096]{0:T(1024)}, u32[]{:S(2)}) copy-start(f32[4096]{0:T(1024)} %param.15) | copy-start | bytes 49156
